TPU v7x, 512 devices: a whole 4x4x16 slice. The times are simulated.
512 devices in a mesh: frame: 32 (over z_hi, y, x), tensor: 16 (over z_lo, core).
Axes of the slice: x: 4, y: 4, z: 16 (z_hi: 2, z_lo: 8; z = z_hi * 8 + z_lo), core: 2. Of those that a mesh axis runs over, the one named last changes fastest.
Arguments:
- tokens: bfloat16 [16384, 1, 4096], P(('frame', 'tensor')), may hold values from -6 to 6
- norm_gain: float32 [4096], replicated, may hold values from 0.5 to 1.5
- query_weight: bfloat16 [4096, 4096], P(None, 'tensor'), may hold values from -0.09375 to 0.09375
- out_weight: bfloat16 [4096, 4096], P('tensor'), may hold values from -0.09375 to 0.09375
- cache_keys: bfloat16 [1536, 1, 4096], P('frame', None, 'tensor'), may hold values from -420 to 420
- cache_values: bfloat16 [1536, 1, 4096], P('frame', None, 'tensor'), may hold values from -18 to 18
- token_pos: int32 [16384, 1], P('frame'), may hold values from 0 to 1535, as said below
- frame_pad: int32 [1], replicated, may hold values from 0 to 768
Outputs:
- mixed: bfloat16 [16384, 1, 4096], P(('frame', 'tensor'))
Inputs may be any that keep to these rules, and one draw needn't show every extreme that they name: `token_pos`: nondecreasing along each sequence; the last token of every sequence has 1535.
All inputs are finite; a program needn't handle non-finite values.
Results may differ from a plain program's by a relative error of at most 0.018.
Values may be sent and summed in bfloat16 or wider, within the bound.
No kernel may reach another device: no remote copies, remote signals or barrier semaphores. Data moves between devices by JAX's collectives and lax.ppermute only.
A program may use at most 64 MiB of HBM per device.

v0:
```python
import jax
import jax.numpy as jnp
from jax import lax
from jax.sharding import PartitionSpec as P

HEAD_DIM = 128
epsilon = 1e-06
masked_score = -1e30


def normalize(block_rows, norm_gain):
    hidden = block_rows.astype(jnp.float32)
    factor = lax.rsqrt(jnp.mean(hidden * hidden, axis=-1, keepdims=True) + epsilon)
    return (hidden * factor * norm_gain).astype(jnp.bfloat16)


def per_device(
    tokens, norm_gain, query_weight, out_weight, cache_keys, cache_values, token_pos, frame_pad
):
    head_cols = query_weight.shape[1]
    heads_here = head_cols // HEAD_DIM
    seq_count = tokens.shape[1]
    query_scale = HEAD_DIM ** (-0.5)
    outgoing = normalize(tokens, norm_gain)
    queries = (
        jnp.dot(
            lax.all_gather(outgoing, "tensor", axis=0, tiled=True),
            query_weight,
            preferred_element_type=jnp.float32,
        )
        * query_scale
    ).astype(jnp.bfloat16)
    query_rows = queries.shape[0]
    query_heads = queries.reshape(query_rows, seq_count, heads_here, HEAD_DIM)
    all_frames = cache_keys.shape[0] * lax.axis_size("frame")
    valid_frames = all_frames - frame_pad
    start_max = jnp.full((query_rows, seq_count, heads_here), masked_score, jnp.float32)
    running_max = start_max
    key_piece = lax.all_gather(cache_keys, "frame", axis=0, tiled=True)
    value_piece = lax.all_gather(cache_values, "frame", axis=0, tiled=True)
    row_count = key_piece.shape[0]
    frame_index = jnp.arange(row_count, dtype=jnp.int32)
    visible = (frame_index[None, None, :] <= token_pos[:, :, None]) & (
        frame_index[None, None, :] < valid_frames[None, :, None]
    )
    key_heads = key_piece.reshape(row_count, seq_count, heads_here, HEAD_DIM)
    scores = jnp.einsum(
        "rshd,fshd->rshf", query_heads, key_heads, preferred_element_type=jnp.float32
    )
    visible = visible[:, :, None, :]
    scores, visible = (jnp.where(visible, scores, masked_score), visible)
    new_max = jnp.maximum(running_max, jnp.max(scores, axis=-1))
    weights = jnp.where(visible, jnp.exp(scores - new_max[..., None]), 0.0)
    running_sum = jnp.sum(weights, axis=-1)
    value_heads = value_piece.reshape(value_piece.shape[0], seq_count, heads_here, HEAD_DIM)
    accumulated = jnp.einsum(
        "rshf,fshd->rshd",
        weights.astype(jnp.bfloat16),
        value_heads,
        preferred_element_type=jnp.float32,
    )
    running_max, running_sum, accumulated = (new_max, running_sum, accumulated)
    attended = (
        (accumulated / running_sum[..., None])
        .astype(jnp.bfloat16)
        .reshape(query_rows, seq_count, head_cols)
    )
    return lax.psum_scatter(
        jnp.dot(attended, out_weight, preferred_element_type=jnp.float32).astype(jnp.bfloat16),
        "tensor",
        scatter_dimension=0,
        tiled=True,
    )


def solution(mesh):
    placed = (
        P(("frame", "tensor"), None, None),
        P(),
        P(None, "tensor"),
        P("tensor", None),
        P("frame", None, "tensor"),
        P("frame", None, "tensor"),
        P("frame", None),
        P(),
    )
    return jax.shard_map(
        per_device,
        mesh=mesh,
        in_specs=placed,
        out_specs=P(("frame", "tensor"), None, None),
        check_vma=False,
    )
```

profile of v0, /device:TPU:12, one launch (start us, length us, event | category | flops | bytes accessed | tf_op | source)
XLA Modules:
  0.0 464.5 jit_solution(3910015531161201871)
XLA Ops:
  6.5 0.0 copy-start
  6.5 0.0 all-gather.2.cloned.1.call-start
  6.5 1.3 fusion.26
  7.8 1.8 fusion.28
  9.6 0.0 all-gather.2.cloned.1.call-update
  9.6 0.0 reduce-scatter.2.cloned.1.call-start
  10.3 132.0 %all_gather.10 = bf16[1536,1,256]{2,0,1:T(8,128)(2,1)S(1)} all-gather(bf16[48,1,256]{2,0,1:T(8,128)(2,1)} %param.12), channel_id=1, replica_groups=mesh['frame'=32,'tensor'=16] {'frame'}, dimensions={0}, use_global_device_ids=true | all-gather | bytes 811008 | tf_op jit(solution)/shard_map/all_gather | solution.py:39
  142.3 1.2 copy.15
  143.5 150.9 %all_gather.11 = bf16[1536,1,256]{2,0,1:T(8,128)(2,1)S(1)} all-gather(bf16[48,1,256]{2,0,1:T(8,128)(2,1)} %param.13), channel_id=1, replica_groups=mesh['frame'=32,'tensor'=16] {'frame'}, dimensions={0}, use_global_device_ids=true | all-gather | bytes 811008 | tf_op jit(solution)/shard_map/all_gather | solution.py:40
  294.4 1.2 copy.18
  295.6 1.3 fusion.9
  296.8 0.0 all-gather.2.cloned.1.call-done
  296.9 0.0 copy-start.1
  296.9 4.2 fusion.17
  301.1 0.0 copy-done.1
  301.1 0.0 copy-start.2
  301.1 1.3 fusion
  302.5 2.0 fusion.2
  304.5 0.0 copy-done.2
  304.5 1.9 fusion.23
  306.4 0.0 copy-done
  306.4 3.2 fusion.1
  309.6 0.0 reduce-scatter.2.cloned.1.call-update
  309.7 148.0 %reduce-scatter.2.cloned.1.call-done = bf16[32,1,4096]{2,0,1:T(8,128)(2,1)} async-done(((bf16[512,1,4096]{2,0,1:T(8,128)(2,1)}), bf16[32,1,4096]{2,0,1:T(8,128)(2,1)}) %reduce-scatter.2.cloned.1.call-update) | async-done | bytes 262160 | tf_op jit(solution)/shard_map/reduce_scatter | solution.py:68
  (3 shorter events, 0.0 us)
Async XLA Ops:
  6.5 299.9 %copy-start = (bf16[256,4096]{1,0:T(8,128)(2,1)S(1)}, bf16[256,4096]{1,0:T(8,128)(2,1)}, u32[]{:S(2)}) copy-start(bf16[256,4096]{1,0:T(8,128)(2,1)} %param.11) | copy-start | bytes 6291460
  6.5 290.3 %all-gather.2.cloned.1.call-start = ((), (), s32[]{:S(2)}) async-start(), calls=%async_computation.1 | async-start | bytes 4456448 | tf_op jit(solution)/shard_map/all_gather | solution.py:27
  9.6 448.0 %reduce-scatter.2.cloned.1.call-start = ((), (), s32[]{:S(2)}) async-start(), calls=%async_computation.2 | async-start | bytes 4456448 | tf_op jit(solution)/shard_map/reduce_scatter | solution.py:68
  296.9 4.2 copy-start.1
  301.1 3.4 copy-start.2
Sparse Core Ops, SparseCore 0:
  9.7 110.9 all-gather.1
  309.8 147.7 reduce-scatter.1
where the time goes:
time: 465 us; the launch traced here: 464 us
  blocking collectives  283 us (61%)
  waiting for transfers between devices  148 us (32%)
  between operations  14.1 us (3%)
  matrix products  10.7 us (2%)
  other arithmetic  6.36 us (1%)
    all_gather x1, blocking collectives, per_device(): value_piece = lax.all_gather(cache_values, 'frame', axis=0, tiled=True)  151 us
    reduce_scatter x1, waiting for transfers between devices, per_device(): lax.psum_scatter(jnp.dot(attended, out_weight, preferred_element_type=jnp...  148 us
    all_gather x1, blocking collectives, per_device(): key_piece = lax.all_gather(cache_keys, 'frame', axis=0, tiled=True)  132 us
  transfers between devices with their start and end apart: 2, of which 1 were waited for; matrix products, arithmetic and copies ran while one was open for 1% of the time, Pallas kernels for 0%

commit v1 on v0

--- a/solution.py
+++ b/solution.py
@@ -36,7 +36,9 @@
     valid_frames = all_frames - frame_pad
     start_max = jnp.full((query_rows, seq_count, heads_here), masked_score, jnp.float32)
     running_max = start_max
-    key_piece = lax.all_gather(cache_keys, "frame", axis=0, tiled=True)
+    key_piece = jnp.concatenate(
+        lax.all_to_all(jnp.stack([cache_keys] * lax.axis_size("frame")), "frame", 0, 0), axis=0
+    )
     value_piece = lax.all_gather(cache_values, "frame", axis=0, tiled=True)
     row_count = key_piece.shape[0]
     frame_index = jnp.arange(row_count, dtype=jnp.int32)

time: 465 us -> 367 us (0.79)
  the two profiles are of different devices: /device:TPU:12 before, /device:TPU:8 now
where the time goes in v1:
time: 367 us
  blocking collectives  164 us (45%)
  waiting for transfers between devices  145 us (40%)
  starting transfers between devices  20.9 us (6%)
  between operations  14.1 us (4%)
  matrix products  10.8 us (3%)
  other arithmetic  6.36 us (2%)
  local copies, waits for them, and re-layouts  5.6 us (2%)
    all_gather x1, blocking collectives, per_device(): value_piece = lax.all_gather(cache_values, 'frame', axis=0, tiled=True)  164 us
    reduce_scatter x1, waiting for transfers between devices, per_device(): lax.psum_scatter(jnp.dot(attended, out_weight, preferred_element_type=jnp...  145 us
    all_to_all x1, starting transfers between devices, per_device(): lax.all_to_all(jnp.stack([cache_keys] * lax.axis_size('frame')), 'frame',...  20.8 us
  transfers between devices with their start and end apart: 3, of which 1 were waited for; matrix products, arithmetic and copies ran while one was open for 2% of the time, Pallas kernels for 0%

profile of v1, /device:TPU:8, one launch (start us, length us, event | category | flops | bytes accessed | tf_op | source)
XLA Modules:
  0.0 366.7 jit_solution(17675113454784994772)
XLA Ops:
  6.5 0.0 copy-start
  6.5 0.0 all-gather.2.cloned.1.call-start
  6.5 1.3 fusion.28
  7.8 1.8 fusion.30
  9.6 0.0 all-gather.2.cloned.1.call-update
  9.6 1.7 stack.2
  11.3 20.8 %all-to-all-start = ((bf16[32,48,1,256]{3,1,2,0:T(8,128)(2,1)}), bf16[32,48,1,256]{3,1,2,0:T(8,128)(2,1)}, u32[]{:S(2)}, u32[]{:S(2)}) async-start(bf16[32,48,1,256]{3,1,2,0:T(8,128)(2,1)} %stack.2), calls=%async_computation | async-start | bytes 1572864 | tf_op jit(solution)/shard_map/all_to_all | solution.py:40
  32.2 0.0 reduce-scatter.2.cloned.1.call-start
  32.9 164.2 %all_gather.7 = bf16[1536,1,256]{2,0,1:T(8,128)(2,1)S(1)} all-gather(bf16[48,1,256]{2,0,1:T(8,128)(2,1)} %param.13), channel_id=1, replica_groups=mesh['frame'=32,'tensor'=16] {'frame'}, dimensions={0}, use_global_device_ids=true | all-gather | bytes 811008 | tf_op jit(solution)/shard_map/all_gather | solution.py:42
  197.1 1.2 copy.16
  198.3 1.3 fusion.9
  199.5 0.0 all-to-all-done
  199.5 2.7 reshape.111
  202.3 4.2 %fusion.17 = bf16[512,256]{0,1:T(8,128)(2,1)S(1)} fusion(bf16[4096,256]{1,0:T(8,128)(2,1)} %param.10, bf16[512,1,4096]{2,0,1:T(8,128)(2,1)} %all-gather.2.cloned.1.call-done), kind=kOutput, calls=%fused_computation.16 | convolution fusion | flops 1074003968 | bytes 6553600 | tf_op jit(solution)/shard_map/dot_general | solution.py:26
  206.5 0.0 copy-done.1
  206.5 0.0 copy-start.2
  206.5 1.5 fusion
  208.0 2.0 fusion.2
  210.1 0.0 copy-done.2
  210.1 1.9 fusion.23
  212.0 0.0 copy-done
  212.0 3.2 fusion.1
  215.2 0.0 reduce-scatter.2.cloned.1.call-update
  215.2 144.6 %reduce-scatter.2.cloned.1.call-done = bf16[32,1,4096]{2,0,1:T(8,128)(2,1)} async-done(((bf16[512,1,4096]{2,0,1:T(8,128)(2,1)}), bf16[32,1,4096]{2,0,1:T(8,128)(2,1)}) %reduce-scatter.2.cloned.1.call-update) | async-done | bytes 262160 | tf_op jit(solution)/shard_map/reduce_scatter | solution.py:70
  (5 shorter events, 0.0 us)
Async XLA Ops:
  6.5 205.5 %copy-start = (bf16[256,4096]{1,0:T(8,128)(2,1)S(1)}, bf16[256,4096]{1,0:T(8,128)(2,1)}, u32[]{:S(2)}) copy-start(bf16[256,4096]{1,0:T(8,128)(2,1)} %param.11) | copy-start | bytes 6291460
  6.5 195.7 %all-gather.2.cloned.1.call-start = ((), (), s32[]{:S(2)}) async-start(), calls=%async_computation.2 | async-start | bytes 4456448 | tf_op jit(solution)/shard_map/all_gather | solution.py:27
  11.3 188.2 %all-to-all-start = ((bf16[32,48,1,256]{3,1,2,0:T(8,128)(2,1)}), bf16[32,48,1,256]{3,1,2,0:T(8,128)(2,1)}, u32[]{:S(2)}, u32[]{:S(2)}) async-start(bf16[32,48,1,256]{3,1,2,0:T(8,128)(2,1)} %stack.2), calls=%async_computation | async-start | bytes 1572864 | tf_op jit(solution)/shard_map/all_to_all | solution.py:40
  32.2 327.7 %reduce-scatter.2.cloned.1.call-start = ((), (), s32[]{:S(2)}) async-start(), calls=%async_computation.3 | async-start | bytes 4456448 | tf_op jit(solution)/shard_map/reduce_scatter | solution.py:70
  202.3 4.2 %copy-start.1 = (bf16[1536,2,128]{2,1,0:T(2,128)(2,1)S(1)}, bf16[1536,2,128]{2,1,0:T(2,128)(2,1)}, u32[]{:S(2)}) copy-start(bf16[1536,2,128]{2,1,0:T(2,128)(2,1)} %reshape.111) | copy-start | bytes 2359300
  206.5 3.6 copy-start.2
Sparse Core Ops, SparseCore 0:
  9.7 131.6 all-gather.1
  215.4 144.4 reduce-scatter.1

commit v2 on v0

--- a/solution.py
+++ b/solution.py
@@ -36,8 +36,13 @@
     valid_frames = all_frames - frame_pad
     start_max = jnp.full((query_rows, seq_count, heads_here), masked_score, jnp.float32)
     running_max = start_max
-    key_piece = lax.all_gather(cache_keys, "frame", axis=0, tiled=True)
-    value_piece = lax.all_gather(cache_values, "frame", axis=0, tiled=True)
+    key_piece, value_piece = jnp.split(
+        lax.all_gather(
+            jnp.concatenate([cache_keys, cache_values], axis=1), "frame", axis=0, tiled=True
+        ),
+        [cache_keys.shape[1]],
+        axis=1,
+    )
     row_count = key_piece.shape[0]
     frame_index = jnp.arange(row_count, dtype=jnp.int32)
     visible = (frame_index[None, None, :] <= token_pos[:, :, None]) & (

time: 465 us -> 367 us (0.79)
  the two profiles are of different devices: /device:TPU:12 before, /device:TPU:8 now
where the time goes in v2:
time: 367 us
  waiting for transfers between devices  320 us (87%)
  local copies, waits for them, and re-layouts  15.8 us (4%)
  between operations  13.8 us (4%)
  matrix products  10.8 us (3%)
  other arithmetic  6.58 us (2%)
    all_gather x1, waiting for transfers between devices, per_device(): lax.all_gather(jnp.concatenate([cache_keys, cache_values], axis=1), 'fram...  123 us
    reduce_scatter x1, waiting for transfers between devices, per_device(): lax.psum_scatter(jnp.dot(attended, out_weight, preferred_element_type=jnp...  113 us
    all_gather x1, waiting for transfers between devices, per_device(): lax.all_gather(outgoing, 'tensor', axis=0, tiled=True)  83.8 us
    split x2, local copies, waits for them, and re-layouts, per_device(): jnp.split(lax.all_gather(jnp.concatenate([cache_keys, cache_values], axis...  10.5 us
  transfers between devices with their start and end apart: 3, of which 3 were waited for; matrix products, arithmetic and copies ran while one was open for 5% of the time, Pallas kernels for 0%

profile of v2, /device:TPU:8, one launch (start us, length us, event | category | flops | bytes accessed | tf_op | source)
XLA Modules:
  0.0 366.8 jit_solution(1972710451527598370)
XLA Ops:
  6.5 0.0 copy-start
  6.5 0.0 all-gather.3.cloned.1.call-start
  6.5 0.9 pad_maximum_fusion
  7.4 0.7 copy.17
  8.1 0.0 all-gather.3.cloned.1.call-update
  8.1 0.0 all-gather.5.cloned.1.call-start
  8.2 1.1 fusion.26
  9.3 1.8 fusion.28
  11.1 0.0 all-gather.5.cloned.1.call-update
  11.1 0.0 reduce-scatter.2.cloned.1.call-start
  11.8 1.3 fusion.9
  13.1 123.0 %all-gather.3.cloned.1.call-done = bf16[1536,2,256]{2,1,0:T(2,128)(2,1)} async-done(((bf16[48,2,256]{2,1,0:T(2,128)(2,1)}), bf16[1536,2,256]{2,1,0:T(2,128)(2,1)}) %all-gather.3.cloned.1.call-update) | async-done | bytes 1572880 | tf_op jit(solution)/shard_map/all_gather | solution.py:40
  136.1 5.8 %fusion.31 = (bf16[1536,1,256]{2,1,0:T(2,128)(2,1)}, bf16[1536,1,256]{2,1,0:T(2,128)(2,1)}) fusion(bf16[1536,2,256]{2,1,0:T(2,128)(2,1)} %all-gather.3.cloned.1.call-done), kind=kLoop, calls=%fused_computation.30 | loop fusion | bytes 3145728 | tf_op jit(solution)/shard_map/split | solution.py:39
  141.9 4.7 %copy.26 = bf16[1536,1,256]{0,2,1:T(8,128)(2,1)} copy(bf16[1536,1,256]{2,1,0:T(2,128)(2,1)} %get-tuple-element.5) | data formatting | bytes 1572864
  146.6 4.7 %copy.18 = bf16[1536,1,256]{0,2,1:T(8,128)(2,1)} copy(bf16[1536,1,256]{2,1,0:T(2,128)(2,1)} %get-tuple-element.6) | data formatting | bytes 1572864 | tf_op jit(solution)/shard_map/split | solution.py:39
  151.3 83.8 %all-gather.5.cloned.1.call-done = bf16[512,1,4096]{2,0,1:T(8,128)(2,1)} async-done(((bf16[32,1,4096]{2,0,1:T(8,128)(2,1)}), bf16[512,1,4096]{2,0,1:T(8,128)(2,1)}) %all-gather.5.cloned.1.call-update) | async-done | bytes 4194320 | tf_op jit(solution)/shard_map/all_gather | solution.py:27
  235.0 4.2 %fusion.17 = bf16[512,256]{0,1:T(8,128)(2,1)S(1)} fusion(bf16[4096,256]{1,0:T(8,128)(2,1)} %param.10, bf16[512,1,4096]{2,0,1:T(8,128)(2,1)} %all-gather.5.cloned.1.call-done), kind=kOutput, calls=%fused_computation.16 | convolution fusion | flops 1074003968 | bytes 6553600 | tf_op jit(solution)/shard_map/dot_general | solution.py:26
  239.2 0.0 copy-done.1
  239.3 1.4 fusion
  240.6 1.5 fusion.2
  242.1 2.0 fusion.23
  244.2 3.2 fusion.1
  247.4 0.0 reduce-scatter.2.cloned.1.call-update
  247.4 112.9 %reduce-scatter.2.cloned.1.call-done = bf16[32,1,4096]{2,0,1:T(8,128)(2,1)} async-done(((bf16[512,1,4096]{2,0,1:T(8,128)(2,1)}), bf16[32,1,4096]{2,0,1:T(8,128)(2,1)}) %reduce-scatter.2.cloned.1.call-update) | async-done | bytes 262160 | tf_op jit(solution)/shard_map/reduce_scatter | solution.py:73
  (7 shorter events, 0.0 us)
Async XLA Ops:
  6.5 237.6 %copy-start = (bf16[256,4096]{1,0:T(8,128)(2,1)S(1)}, bf16[256,4096]{1,0:T(8,128)(2,1)}, u32[]{:S(2)}) copy-start(bf16[256,4096]{1,0:T(8,128)(2,1)} %param.11) | copy-start | bytes 6291460
  6.5 129.5 %all-gather.3.cloned.1.call-start = ((), (), s32[]{:S(2)}) async-start(), calls=%async_computation.1 | async-start | bytes 1622016 | tf_op jit(solution)/shard_map/all_gather | solution.py:40
  8.1 226.9 %all-gather.5.cloned.1.call-start = ((), (), s32[]{:S(2)}) async-start(), calls=%async_computation.2 | async-start | bytes 4456448 | tf_op jit(solution)/shard_map/all_gather | solution.py:27
  11.1 349.1 %reduce-scatter.2.cloned.1.call-start = ((), (), s32[]{:S(2)}) async-start(), calls=%async_computation.3 | async-start | bytes 4456448 | tf_op jit(solution)/shard_map/reduce_scatter | solution.py:73
  235.0 4.2 %copy-start.1 = (bf16[1536,1,256]{0,2,1:T(8,128)(2,1)S(1)}, bf16[1536,1,256]{0,2,1:T(8,128)(2,1)}, u32[]{:S(2)}) copy-start(bf16[1536,1,256]{0,2,1:T(8,128)(2,1)} %copy.26) | copy-start | bytes 2359300
  240.6 1.5 copy-start.2
Sparse Core Ops, SparseCore 0:
  11.7 124.3 all-gather.2
  138.2 96.8 all-gather.4
  247.5 112.6 reduce-scatter.1
